TPU v7x, 32 devices: a whole 2x2x4 slice. The times are simulated.
32 devices in a mesh: tm: 16 (over z, y, core), mp: 2 (over x).
Axes of the slice: x: 2, y: 2, z: 4, core: 2. Of those that a mesh axis runs over, the one named last changes fastest.
Arguments:
- latent_picture_tokens: bfloat16 [32, 384, 768], P(('tm', 'mp')), may hold values from -6 to 6
- mixing_rescale_factor: float32 [2, 768], replicated, may hold values from 0.1 to 1.9
- joint_lookup_matrix: bfloat16 [2, 768, 1280], P(None, None, 'mp')
- score_scaling: float32 [2, 6], replicated, may hold values from 1 to 24
- mixing_return_matrix: bfloat16 [2, 768, 768], P(None, 'mp'), may hold values from -0.21875 to 0.21875
- perceptron_rescale_factor: float32 [2, 768], replicated, may hold values from 0.1 to 1.9
- widening_matrix: bfloat16 [2, 768, 1536], P(None, None, 'mp'), may hold values from -0.21875 to 0.21875
- narrowing_matrix: bfloat16 [2, 1536, 768], P(None, 'mp'), may hold values from -0.15625 to 0.15625
Outputs:
- result: bfloat16 [32, 384, 768], P(('tm', 'mp'))
All inputs are finite; a program needn't handle non-finite values.
Results may differ from a plain program's by a relative error of at most 0.033.
Values may be sent and summed in bfloat16 or wider, within the bound.
A program may use at most 128 MiB of HBM per device.

v0:
```python
import math

import jax
import jax.numpy as jnp
from jax import lax
from jax.sharding import PartitionSpec as P

HEAD_SIZE = 128
ASKERS_IN_GROUP = 3
S = 384


def passed_along(value, axis, by):
    size = lax.axis_size(axis)
    pairs = [(i, i + by) for i in range(size) if 0 <= i + by < size]
    return lax.ppermute(value, axis, pairs)


def from_root(value, axis, root):
    mine = lax.axis_index(axis) == root
    return lax.psum(jnp.where(mine, value, jnp.zeros_like(value)), axis)


def rms_rows(x, gain):
    content_vectors = x.astype(jnp.float32)
    scale = lax.rsqrt(jnp.mean(content_vectors * content_vectors, axis=-1, keepdims=True) + 1e-06)
    return content_vectors * scale * gain


def head_norm(t):
    return t * lax.rsqrt(jnp.mean(t * t, axis=-1, keepdims=True) + 1e-06)


def separate_subspaces(flat_vectors, groups, temps):
    count = flat_vectors.shape[0]
    reshaped_rows = flat_vectors.reshape(count, S, groups, ASKERS_IN_GROUP + 2, HEAD_SIZE)
    asker_vectors = (
        head_norm(reshaped_rows[:, :, :, :ASKERS_IN_GROUP, :])
        * temps[None, None, :, :, None]
        / math.sqrt(HEAD_SIZE)
    )
    matcher_vectors = head_norm(reshaped_rows[:, :, :, ASKERS_IN_GROUP, :])
    content_vectors = reshaped_rows[:, :, :, ASKERS_IN_GROUP + 1, :]
    return (
        asker_vectors.astype(jnp.bfloat16),
        matcher_vectors.astype(jnp.bfloat16),
        content_vectors.astype(jnp.bfloat16),
    )


def attend(
    asker_vectors, matcher_vectors, content_vectors, prior_k, prior_v, anchor_k, anchor_v, frame_ids
):
    own = jnp.einsum(
        "fsgrd,ftgd->fgrst", asker_vectors, matcher_vectors, preferred_element_type=jnp.float32
    )
    prior = jnp.einsum(
        "fsgrd,ftgd->fgrst", asker_vectors, prior_k, preferred_element_type=jnp.float32
    )
    anchor = jnp.einsum(
        "fsgrd,tgd->fgrst", asker_vectors, anchor_k, preferred_element_type=jnp.float32
    )
    lowest = jnp.float32(-1e30)
    prior = jnp.where((frame_ids >= 1)[:, None, None, None, None], prior, lowest)
    anchor = jnp.where((frame_ids >= 2)[:, None, None, None, None], anchor, lowest)
    top = jnp.maximum(
        jnp.maximum(jnp.max(own, axis=-1, keepdims=True), jnp.max(prior, axis=-1, keepdims=True)),
        jnp.max(anchor, axis=-1, keepdims=True),
    )
    e_own = jnp.exp(own - top)
    e_prior = jnp.exp(prior - top)
    e_anchor = jnp.exp(anchor - top)
    total = (
        jnp.sum(e_own, axis=-1, keepdims=True)
        + jnp.sum(e_prior, axis=-1, keepdims=True)
        + jnp.sum(e_anchor, axis=-1, keepdims=True)
    )
    p_own = (e_own / total).astype(jnp.bfloat16)
    p_prior = (e_prior / total).astype(jnp.bfloat16)
    p_anchor = (e_anchor / total).astype(jnp.bfloat16)
    mixed = jnp.einsum(
        "fgrst,ftgd->fsgrd", p_own, content_vectors, preferred_element_type=jnp.float32
    )
    mixed = mixed + jnp.einsum(
        "fgrst,ftgd->fsgrd", p_prior, prior_v, preferred_element_type=jnp.float32
    )
    mixed = mixed + jnp.einsum(
        "fgrst,tgd->fsgrd", p_anchor, anchor_v, preferred_element_type=jnp.float32
    )
    count = asker_vectors.shape[0]
    return mixed.astype(jnp.bfloat16).reshape(count, S, -1)


def layer_by_heads(state, gain_attn, qkv_local, temps, out_local, gain_ffn, up_local, down_local):
    groups = qkv_local.shape[1] // ((ASKERS_IN_GROUP + 2) * HEAD_SIZE)
    normed = rms_rows(lax.all_gather(state, "mp", axis=0, tiled=True), gain_attn).astype(
        jnp.bfloat16
    )
    flat_vectors = jnp.einsum("fsd,dc->fsc", normed, qkv_local, preferred_element_type=jnp.float32)
    count = flat_vectors.shape[0]
    local_temps = lax.dynamic_slice_in_dim(
        temps.reshape(-1, ASKERS_IN_GROUP), lax.axis_index("mp") * groups, groups, 0
    )
    asker_vectors, matcher_vectors, content_vectors = separate_subspaces(
        flat_vectors, groups, local_temps
    )
    edge_k, edge_v = passed_along((matcher_vectors[count - 1], content_vectors[count - 1]), "tm", 1)
    prior_k = jnp.concatenate([edge_k[None], matcher_vectors[: count - 1]], axis=0)
    prior_v = jnp.concatenate([edge_v[None], content_vectors[: count - 1]], axis=0)
    anchor_k, anchor_v = (
        from_root(matcher_vectors[0], "tm", 0),
        from_root(content_vectors[0], "tm", 0),
    )
    frame_ids = lax.axis_index("tm") * count + jnp.arange(count, dtype=jnp.int32)
    heads_out = attend(
        asker_vectors,
        matcher_vectors,
        content_vectors,
        prior_k,
        prior_v,
        anchor_k,
        anchor_v,
        frame_ids,
    )
    block = heads_out
    mixed = lax.psum_scatter(
        jnp.einsum("fsc,cd->fsd", block, out_local, preferred_element_type=jnp.float32).astype(
            jnp.bfloat16
        ),
        "mp",
        scatter_dimension=0,
        tiled=True,
    ).astype(jnp.float32)
    state = (state.astype(jnp.float32) + mixed).astype(jnp.bfloat16)
    normed = rms_rows(lax.all_gather(state, "mp", axis=0, tiled=True), gain_ffn).astype(
        jnp.bfloat16
    )
    hidden = jnp.einsum("fsd,dc->fsc", normed, up_local, preferred_element_type=jnp.float32)
    active = jax.nn.gelu(hidden, approximate=True).astype(jnp.bfloat16)
    block = active
    update = lax.psum_scatter(
        jnp.einsum("fsc,cd->fsd", block, down_local, preferred_element_type=jnp.float32).astype(
            jnp.bfloat16
        ),
        "mp",
        scatter_dimension=0,
        tiled=True,
    ).astype(jnp.float32)
    return (state.astype(jnp.float32) + update).astype(jnp.bfloat16)


def shards(
    latent_picture_tokens,
    mixing_rescale_factor,
    joint_lookup_matrix,
    score_scaling,
    mixing_return_matrix,
    perceptron_rescale_factor,
    widening_matrix,
    narrowing_matrix,
):
    state = latent_picture_tokens
    for depth_position in range(joint_lookup_matrix.shape[0]):
        state = layer_by_heads(
            state,
            mixing_rescale_factor[depth_position],
            joint_lookup_matrix[depth_position],
            score_scaling[depth_position],
            mixing_return_matrix[depth_position],
            perceptron_rescale_factor[depth_position],
            widening_matrix[depth_position],
            narrowing_matrix[depth_position],
        )
    return state


def solution(mesh):
    in_specs = (
        P(("tm", "mp"), None, None),
        P(),
        P(None, None, "mp"),
        P(),
        P(None, "mp", None),
        P(),
        P(None, None, "mp"),
        P(None, "mp", None),
    )
    out_specs = P(("tm", "mp"), None, None)
    return jax.shard_map(shards, mesh=mesh, in_specs=in_specs, out_specs=out_specs, check_vma=False)
```

profile of v0, /device:TPU:29, one launch (start us, length us, event | category | flops | bytes accessed | tf_op | source)
XLA Modules:
  0.0 436.5 jit_solution(16473316181663037896)
XLA Ops:
  6.5 0.7 all-gather.5.cloned.1.call-update
  7.3 2.6 slice_bitcast_fusion.1
  10.0 0.6 copy.36
  10.6 0.6 slice_reduce_fusion.4
  11.3 0.5 fusion.153
  11.8 0.6 slice_reduce_fusion.1
  12.4 20.2 %all-gather.5.cloned.1.call-done = bf16[2,384,768]{2,1,0:T(8,128)(2,1)} async-done(((bf16[1,384,768]{2,1,0:T(8,128)(2,1)}), bf16[2,384,768]{2,1,0:T(8,128)(2,1)}) %all-gather.5.cloned.1.call-update) | async-done | bytes 1179664 | tf_op jit(solution)/shard_map/all_gather | solution.py:96
  32.6 1.6 fusion.12
  34.2 2.3 fusion.88
  36.8 0.9 fusion.121
  37.9 0.7 bitcast_reduce_fusion.5
  38.7 0.7 slice_bitcast_fusion.6
  39.4 0.6 select_bitcast_fusion.2
  40.1 0.7 select_bitcast_fusion.3
  40.9 1.5 slice_bitcast_fusion.7
  42.4 1.3 collective-permute-start
  43.7 1.3 collective-permute-start.1
  45.0 83.3 %all-reduce.7.cloned.1.call-done = (bf16[384,128]{0,1:T(8,128)(2,1)}, bf16[384,128]{0,1:T(8,128)(2,1)}) async-done(((bf16[384,128]{0,1:T(8,128)(2,1)}, bf16[384,128]{0,1:T(8,128)(2,1)}), (bf16[384,128]{0,1:T(8,128)(2,1)}, bf16[384,128]{0,1:T(8,128)(2,1)})) %all-reduce.7.cloned.1.call-update) | async-done | bytes 196624 | tf_op jit(solution)/shard_map/psum | solution.py:21
  128.2 1.8 bitcast_reduce_fusion.3
  130.1 1.6 bitcast_reduce_fusion.4
  131.7 1.7 fusion.8
  133.5 1.8 fusion.50
  135.3 2.0 fusion.67
  137.3 1.0 fusion.76
  138.4 0.2 copy-done.24
  138.6 1.8 convolution_convert_fusion.3
  140.5 23.5 %reduce-scatter.5.cloned.1.call-done = bf16[1,384,768]{2,1,0:T(8,128)(2,1)} async-done(((bf16[2,384,768]{2,1,0:T(8,128)(2,1)}), bf16[1,384,768]{2,1,0:T(8,128)(2,1)}) %reduce-scatter.5.cloned.1.call-update) | async-done | bytes 589840 | tf_op jit(solution)/shard_map/reduce_scatter | solution.py:126
  164.0 2.0 add_convert_fusion.3
  166.0 0.2 reduce-scatter.7.cloned.1.call-start
  166.3 0.6 slice_reduce_fusion
  166.9 22.1 %all-gather.7.cloned.1.call-done = bf16[2,384,768]{2,1,0:T(8,128)(2,1)} async-done(((bf16[1,384,768]{2,1,0:T(8,128)(2,1)}), bf16[2,384,768]{2,1,0:T(8,128)(2,1)}) %all-gather.7.cloned.1.call-update) | async-done | bytes 1179664 | tf_op jit(solution)/shard_map/all_gather | solution.py:135
  189.0 1.6 fusion.15
  190.6 5.4 %convolution_convert_fusion.2 = bf16[2,384,768]{2,1,0:T(8,128)(2,1)} fusion(bf16[2,768,768]{2,1,0:T(8,128)(2,1)} %param.15, bf16[2,384,768]{2,1,0:T(8,128)(2,1)} %all-gather.7.cloned.1.call-done, bf16[2,768,768]{2,1,0:T(8,128)(2,1)} %param.14, f32[768]{0:T(1024)S(1)} %get-tuple-element.12, f32[2,384]{1,0:T(2,128)S(1)} %add_rsqrt_fusion.5), kind=kOutput, calls=%fused_computation.86 | convolution fusion | flops 1820196864 | bytes 4724736 | tf_op jit(solution)/shard_map/fsc,cd->fsd/dot_general | solution.py:142
  196.1 21.8 %reduce-scatter.7.cloned.1.call-done = bf16[1,384,768]{2,1,0:T(8,128)(2,1)} async-done(((bf16[2,384,768]{2,1,0:T(8,128)(2,1)}), bf16[1,384,768]{2,1,0:T(8,128)(2,1)}) %reduce-scatter.7.cloned.1.call-update) | async-done | bytes 589840 | tf_op jit(solution)/shard_map/reduce_scatter | solution.py:141
  217.9 2.0 add_convert_fusion.2
  220.0 0.6 copy.50
  220.7 22.1 %all-gather.9.cloned.1.call-done = bf16[2,384,768]{2,1,0:T(8,128)(2,1)} async-done(((bf16[1,384,768]{2,1,0:T(8,128)(2,1)}), bf16[2,384,768]{2,1,0:T(8,128)(2,1)}) %all-gather.9.cloned.1.call-update) | async-done | bytes 1179664 | tf_op jit(solution)/shard_map/all_gather | solution.py:96
  242.9 1.6 fusion.18
  244.5 2.3 fusion.84
  247.0 0.9 fusion.182
  248.0 0.6 select_bitcast_fusion
  248.6 0.7 slice_bitcast_fusion.3
  249.6 0.7 bitcast_reduce_fusion.2
  250.3 0.7 select_bitcast_fusion.1
  251.0 1.6 slice_bitcast_fusion.4
  252.6 1.3 collective-permute-start.2
  253.9 1.3 collective-permute-start.3
  255.2 83.2 %all-reduce.5.cloned.1.call-done = (bf16[384,128]{0,1:T(8,128)(2,1)}, bf16[384,128]{0,1:T(8,128)(2,1)}) async-done(((bf16[384,128]{0,1:T(8,128)(2,1)}, bf16[384,128]{0,1:T(8,128)(2,1)}), (bf16[384,128]{0,1:T(8,128)(2,1)}, bf16[384,128]{0,1:T(8,128)(2,1)})) %all-reduce.5.cloned.1.call-update) | async-done | bytes 196624 | tf_op jit(solution)/shard_map/psum | solution.py:21
  338.4 1.8 bitcast_reduce_fusion
  340.2 1.6 bitcast_reduce_fusion.1
  341.8 1.7 fusion.10
  343.6 1.8 fusion.44
  345.4 2.0 fusion.73
  347.5 1.0 fusion.79
  348.5 0.2 copy-done.25
  348.7 1.8 convolution_convert_fusion.1
  350.6 23.5 %reduce-scatter.9.cloned.1.call-done = bf16[1,384,768]{2,1,0:T(8,128)(2,1)} async-done(((bf16[2,384,768]{2,1,0:T(8,128)(2,1)}), bf16[1,384,768]{2,1,0:T(8,128)(2,1)}) %reduce-scatter.9.cloned.1.call-update) | async-done | bytes 589840 | tf_op jit(solution)/shard_map/reduce_scatter | solution.py:126
  374.1 2.0 add_convert_fusion.1
  376.1 0.3 reduce-scatter.11.cloned.1.call-start
  376.4 22.7 %all-gather.11.cloned.1.call-done = bf16[2,384,768]{2,1,0:T(8,128)(2,1)} async-done(((bf16[1,384,768]{2,1,0:T(8,128)(2,1)}), bf16[2,384,768]{2,1,0:T(8,128)(2,1)}) %all-gather.11.cloned.1.call-update) | async-done | bytes 1179664 | tf_op jit(solution)/shard_map/all_gather | solution.py:135
  399.1 1.6 fusion.21
  400.7 5.1 %convolution_convert_fusion = bf16[2,384,768]{2,1,0:T(8,128)(2,1)} fusion(bf16[2,768,768]{2,1,0:T(8,128)(2,1)S(1)} %copy-done.23, bf16[2,384,768]{2,1,0:T(8,128)(2,1)} %all-gather.11.cloned.1.call-done, bf16[2,768,768]{2,1,0:T(8,128)(2,1)} %param.14, f32[768]{0:T(1024)S(1)} %copy-done.19, f32[2,384]{1,0:T(2,128)S(1)} %add_rsqrt_fusion.2), kind=kOutput, calls=%fused_computation.84 | convolution fusion | flops 1820196864 | bytes 4725760 | tf_op jit(solution)/shard_map/fsc,cd->fsd/dot_general | solution.py:142
  405.8 21.9 %reduce-scatter.11.cloned.1.call-done = bf16[1,384,768]{2,1,0:T(8,128)(2,1)} async-done(((bf16[2,384,768]{2,1,0:T(8,128)(2,1)}), bf16[1,384,768]{2,1,0:T(8,128)(2,1)}) %reduce-scatter.11.cloned.1.call-update) | async-done | bytes 589840 | tf_op jit(solution)/shard_map/reduce_scatter | solution.py:141
  427.7 2.0 add_convert_fusion
  (102 shorter events, 1.8 us)
Async XLA Ops:
  6.5 26.1 %all-gather.5.cloned.1.call-start = ((), (), s32[]{:S(2)}) async-start(), calls=%async_computation.4 | async-start | bytes 1769472 | tf_op jit(solution)/shard_map/all_gather | solution.py:96
  7.3 121.0 %all-reduce.7.cloned.1.call-start = ((), (), s32[]{:S(2)}) async-start(), calls=%async_computation.13 | async-start | bytes 393216 | tf_op jit(solution)/shard_map/psum | solution.py:21
  7.3 3.3 copy-start.21
  7.3 4.5 %copy-start.17 = (f32[2,768]{1,0:T(2,128)S(1)}, f32[2,768]{1,0:T(2,128)}, u32[]{:S(2)}) copy-start(f32[2,768]{1,0:T(2,128)} %param.9) | copy-start | bytes 18436
  36.6 2.1 copy-start.5
  37.9 0.8 copy-start
  40.8 123.2 %reduce-scatter.5.cloned.1.call-start = ((), (), s32[]{:S(2)}) async-start(), calls=%async_computation.5 | async-start | bytes 1769472 | tf_op jit(solution)/shard_map/reduce_scatter | solution.py:126
  42.4 87.7 %collective-permute-start = (bf16[384,1,128]{0,2,1:T(8,128)(2,1)}, bf16[384,1,128]{0,2,1:T(8,128)(2,1)}, u32[]{:S(2)}, u32[]{:S(2)}) collective-permute-start(bf16[384,1,128]{0,2,1:T(8,128)(2,1)} %slice_bitcast_fusion.7), channel_id=1, source_target_pairs={{0,2},{2,4},{4,6},{6,8},{8,10},{10,12},{12,14},{14,16},{16,18},{18... | collective-permute-start | bytes 294920 | tf_op jit(solution)/shard_map/ppermute | solution.py:16
  43.7 91.6 %collective-permute-start.1 = (bf16[384,1,128]{0,2,1:T(8,128)(2,1)}, bf16[384,1,128]{0,2,1:T(8,128)(2,1)}, u32[]{:S(2)}, u32[]{:S(2)}) collective-permute-start(bf16[384,1,128]{0,2,1:T(8,128)(2,1)} %get-tuple-element.27), channel_id=1, source_target_pairs={{0,2},{2,4},{4,6},{6,8},{8,10},{10,12},{12,14},{14,16},{16,18},{18... | collective-permute-start | bytes 294920 | tf_op jit(solution)/shard_map/ppermute | solution.py:16
  128.2 1.9 copy-start.1
  128.2 1.9 copy-start.12
  130.1 1.6 copy-start.15
  133.5 1.8 copy-start.14
  135.3 2.0 copy-start.27
  137.3 1.3 copy-start.24
  138.4 25.6 %copy-start.10 = (bf16[1,384,768]{2,1,0:T(8,128)(2,1)S(1)}, bf16[1,384,768]{2,1,0:T(8,128)(2,1)}, u32[]{:S(2)}) copy-start(bf16[1,384,768]{2,1,0:T(8,128)(2,1)} %param.8) | copy-start | bytes 1769476
  140.4 25.8 %copy-start.18 = (f32[2,768]{1,0:T(2,128)S(1)}, f32[2,768]{1,0:T(2,128)}, u32[]{:S(2)}) copy-start(f32[2,768]{1,0:T(2,128)} %param.13) | copy-start | bytes 18436
  140.4 48.5 %all-gather.7.cloned.1.call-start = ((), (), s32[]{:S(2)}) async-start(), calls=%async_computation.6 | async-start | bytes 1769472 | tf_op jit(solution)/shard_map/all_gather | solution.py:135
  166.0 51.9 %reduce-scatter.7.cloned.1.call-start = ((), (), s32[]{:S(2)}) async-start(), calls=%async_computation.7 | async-start | bytes 1769472 | tf_op jit(solution)/shard_map/reduce_scatter | solution.py:141
  190.6 27.3 %copy-start.7 = (bf16[1,384,768]{2,1,0:T(8,128)(2,1)S(1)}, bf16[1,384,768]{2,1,0:T(8,128)(2,1)}, u32[]{:S(2)}) copy-start(bf16[1,384,768]{2,1,0:T(8,128)(2,1)} %add_convert_fusion.3) | copy-start | bytes 1769476
  196.0 24.0 %copy-start.9 = (bf16[640,768]{0,1:T(8,128)(2,1)S(1)}, bf16[640,768]{0,1:T(8,128)(2,1)}, u32[]{:S(2)}) copy-start(bf16[640,768]{0,1:T(8,128)(2,1)} %get-tuple-element.22) | copy-start | bytes 2949124
  196.0 24.7 %copy-start.22 = (f32[6]{0:T(128)S(1)}, f32[6]{0:T(128)}, u32[]{:S(2)}) copy-start(f32[6]{0:T(128)} %get-tuple-element.15) | copy-start | bytes 76
  196.0 48.5 %copy-start.20 = (f32[768]{0:T(1024)S(1)}, f32[768]{0:T(1024)}, u32[]{:S(2)}) copy-start(f32[768]{0:T(1024)} %get-tuple-element.13) | copy-start | bytes 9220
  196.0 46.9 %all-gather.9.cloned.1.call-start = ((), (), s32[]{:S(2)}) async-start(), calls=%async_computation.8 | async-start | bytes 1769472 | tf_op jit(solution)/shard_map/all_gather | solution.py:96
  219.9 118.4 %all-reduce.5.cloned.1.call-start = ((), (), s32[]{:S(2)}) async-start(), calls=%async_computation.12 | async-start | bytes 393216 | tf_op jit(solution)/shard_map/psum | solution.py:21
  246.8 2.7 copy-start.4
  249.6 1.4 copy-start.2
  251.0 123.1 %reduce-scatter.9.cloned.1.call-start = ((), (), s32[]{:S(2)}) async-start(), calls=%async_computation.9 | async-start | bytes 1769472 | tf_op jit(solution)/shard_map/reduce_scatter | solution.py:126
  252.6 87.6 %collective-permute-start.2 = (bf16[384,1,128]{0,2,1:T(8,128)(2,1)}, bf16[384,1,128]{0,2,1:T(8,128)(2,1)}, u32[]{:S(2)}, u32[]{:S(2)}) collective-permute-start(bf16[384,1,128]{0,2,1:T(8,128)(2,1)} %slice_bitcast_fusion.4), channel_id=1, source_target_pairs={{0,2},{2,4},{4,6},{6,8},{8,10},{10,12},{12,14},{14,16},{16,18},{18... | collective-permute-start | bytes 294920 | tf_op jit(solution)/shard_map/ppermute | solution.py:16
  253.9 91.5 %collective-permute-start.3 = (bf16[384,1,128]{0,2,1:T(8,128)(2,1)}, bf16[384,1,128]{0,2,1:T(8,128)(2,1)}, u32[]{:S(2)}, u32[]{:S(2)}) collective-permute-start(bf16[384,1,128]{0,2,1:T(8,128)(2,1)} %get-tuple-element.23), channel_id=1, source_target_pairs={{0,2},{2,4},{4,6},{6,8},{8,10},{10,12},{12,14},{14,16},{16,18},{18... | collective-permute-start | bytes 294920 | tf_op jit(solution)/shard_map/ppermute | solution.py:16
  338.3 1.9 copy-start.3
  338.3 1.9 copy-start.11
  340.2 1.6 copy-start.16
  343.6 1.8 copy-start.13
  345.4 2.0 copy-start.26
  347.4 1.3 copy-start.25
  348.5 25.6 %copy-start.6 = (bf16[1,384,768]{2,1,0:T(8,128)(2,1)S(1)}, bf16[1,384,768]{2,1,0:T(8,128)(2,1)}, u32[]{:S(2)}) copy-start(bf16[1,384,768]{2,1,0:T(8,128)(2,1)} %add_convert_fusion.2) | copy-start | bytes 1769476
  350.5 50.1 %copy-start.19 = (f32[768]{0:T(1024)S(1)}, f32[768]{0:T(1024)}, u32[]{:S(2)}) copy-start(f32[768]{0:T(1024)} %get-tuple-element.11) | copy-start | bytes 9220
  350.5 50.2 %copy-start.23 = (bf16[2,768,768]{2,1,0:T(8,128)(2,1)S(1)}, bf16[2,768,768]{2,1,0:T(8,128)(2,1)}, u32[]{:S(2)}) copy-start(bf16[2,768,768]{2,1,0:T(8,128)(2,1)} %param.15) | copy-start | bytes 7077892
  350.6 48.5 %all-gather.11.cloned.1.call-start = ((), (), s32[]{:S(2)}) async-start(), calls=%async_computation.10 | async-start | bytes 1769472 | tf_op jit(solution)/shard_map/all_gather | solution.py:135
  376.1 51.5 %reduce-scatter.11.cloned.1.call-start = ((), (), s32[]{:S(2)}) async-start(), calls=%async_computation.11 | async-start | bytes 1769472 | tf_op jit(solution)/shard_map/reduce_scatter | solution.py:141
  400.7 27.0 %copy-start.8 = (bf16[1,384,768]{2,1,0:T(8,128)(2,1)S(1)}, bf16[1,384,768]{2,1,0:T(8,128)(2,1)}, u32[]{:S(2)}) copy-start(bf16[1,384,768]{2,1,0:T(8,128)(2,1)} %add_convert_fusion.1) | copy-start | bytes 1769476
Sparse Core Ops, SparseCore 0:
  8.9 23.6 all-gather.4
  40.9 87.2 all-reduce.6
  140.6 23.3 reduce-scatter.4
  166.1 22.7 all-gather.6
  196.1 21.7 reduce-scatter.6
  220.0 22.7 all-gather.8
  251.1 87.2 all-reduce.4
  350.7 23.3 reduce-scatter.8
  376.2 22.7 all-gather.10
  405.9 21.7 reduce-scatter.10
where the time goes:
time: 439 us; the launch traced here: 437 us
  waiting for transfers between devices  345 us (79%)
  matrix products  36.6 us (8%)
  other arithmetic  23.7 us (5%)
  between operations  14.1 us (3%)
  local copies, waits for them, and re-layouts  11 us (3%)
  starting transfers between devices  5.92 us (1%)
    psum x2, waiting for transfers between devices, from_root(): return lax.psum(jnp.where(mine, value, jnp.zeros_like(value)), axis)  166 us
    all_gather x4, waiting for transfers between devices, layer_by_heads(): lax.all_gather(state, 'mp', axis=0, tiled=True)  87.1 us
    reduce_scatter x2, waiting for transfers between devices, layer_by_heads(): lax.psum_scatter(jnp.einsum('fsc,cd->fsd', block, out_local, preferred_el...  47 us
    reduce_scatter x2, waiting for transfers between devices, layer_by_heads(): lax.psum_scatter(jnp.einsum('fsc,cd->fsd', block, down_local, preferred_e...  43.7 us
    dot_general x2, matrix products, layer_by_heads(): jnp.einsum('fsc,cd->fsd', block, down_local, preferred_element_type=jnp.f...  10.4 us
  transfers between devices with their start and end apart: 14, of which 10 were waited for; matrix products, arithmetic and copies ran while one was open for 5% of the time, Pallas kernels for 0%

commit v1 on v0

v1 whole, which is shorter than its diff:
```python
import math

import jax
import jax.numpy as jnp
from jax import lax
from jax.experimental import pallas as pl
from jax.experimental.pallas import tpu as pltpu
from jax.sharding import PartitionSpec as P

D = 128
R = 3
S = 384
XCH = 4
MESH = pl.DeviceIdType.MESH
F32, BF16 = jnp.float32, jnp.bfloat16


def norm_rows(x, gain):
    x = x.astype(F32)
    scale = lax.rsqrt(jnp.mean(x * x, axis=-1, keepdims=True) + 1e-06)
    return (x * scale * gain).astype(BF16)


def head_norm(t):
    return t * lax.rsqrt(jnp.mean(t * t, axis=-1, keepdims=True) + 1e-06)


def dot(a, b):
    return jnp.dot(a, b, preferred_element_type=F32)


def kernel(
    T,
    x_ref, ga_ref, qkv_ref, temp_ref, out_ref, gf_ref, up_ref, down_ref,
    y_ref,
    wq, wo, wu, wd, x0, st, h, q, kc, vc, o, act,
    ws, wr, xsend, xrecv, ksend, krecv,
):
    tm, mp = lax.axis_index("tm"), lax.axis_index("mp")
    c, yb, zb = lax.rem(tm, 2), lax.rem(tm // 2, 2), lax.rem(tm // 4, 2)
    frame = tm * 2 + mp
    xdev = (tm, 1 - mp)
    cdev = (tm + 1 - 2 * c, mp)
    ydev = (tm + 2 - 4 * yb, mp)
    zdev = (tm + 4 - 8 * zb, mp)
    has_next = frame < 2 * T - 1
    has_prev = frame > 0
    ndev = (jnp.minimum(tm + mp, T - 1), 1 - mp)
    chain = jnp.logical_and(lax.rem(tm, 4) == 0, mp == 0)
    chain_next = jnp.logical_and(chain, tm + 4 < T)
    znext = jnp.minimum(tm + 4, T - 4)

    barrier = pltpu.get_barrier_semaphore()
    for dev in (xdev, cdev, ydev, zdev):
        pl.semaphore_signal(barrier, inc=1, device_id=dev, device_id_type=MESH)
    diag_up = jnp.logical_and(mp == 1, tm < T - 1)
    diag_down = jnp.logical_and(mp == 0, tm > 0)
    z_up = jnp.logical_and(jnp.logical_and(chain, zb == 1), tm + 4 < T)
    z_down = jnp.logical_and(jnp.logical_and(chain, zb == 0), tm > 0)

    def greet(cond, dev):
        @pl.when(cond)
        def _():
            pl.semaphore_signal(barrier, inc=1, device_id=dev, device_id_type=MESH)

    greet(diag_up, (jnp.minimum(tm + 1, T - 1), 0))
    greet(diag_down, (jnp.maximum(tm - 1, 0), 1))
    greet(z_up, (znext, 0))
    greet(z_down, (jnp.maximum(tm - 4, 0), 0))
    peers = jnp.int32(4)
    for cond in (diag_up, diag_down, z_up, z_down):
        peers = peers + jnp.where(cond, 1, 0)
    pl.semaphore_wait(barrier, peers)

    mats = []
    for l in range(2):
        mats += [(qkv_ref, wq, l), (out_ref, wo, l), (up_ref, wu, l), (down_ref, wd, l)]

    def wcopy(m, stage):
        src, dst, l = mats[m]
        rows = dst.shape[1] // 8
        y_first = m % 2 == 0
        e = c * 4 + (zb * 2 + yb if y_first else yb * 2 + zb)
        if stage == 0:
            at = pl.ds(pl.multiple_of(e * rows, rows), rows)
            sref, dev = src.at[l, at], xdev
        else:
            n = (0, 1, 2, 4)[stage]
            lead = (e, e, c * 4 + (zb if y_first else yb) * 2, c * 4)[stage]
            at = pl.ds(pl.multiple_of(lead * rows, rows), n * rows)
            sref = dst.at[l, at]
            dev = (None, ydev if y_first else zdev, zdev if y_first else ydev, cdev)[stage]
        return pltpu.make_async_remote_copy(
            src_ref=sref, dst_ref=dst.at[l, at], send_sem=ws.at[m, stage],
            recv_sem=wr.at[m, stage], device_id=dev, device_id_type=MESH,
        )

    def tick(t):
        if t + 2 < 8:
            wcopy(t + 2, 0).start()
        for stage in (1, 2, 3):
            m = t + 1 - stage
            if 0 <= m < 8:
                wcopy(m, stage - 1).wait_recv()
                wcopy(m, stage).start()

    def arrived(m):
        wcopy(m, 3).wait_recv()

    step = S // XCH
    children = (
        (chain_next, (znext, 0)),
        (chain, (tm + 2 - 4 * yb, 0)),
        (jnp.logical_and(c == 0, mp == 0), (tm, 1)),
        (c == 0, cdev),
    )

    def xcopy(k, child, src):
        at = pl.ds(k * step, step)
        return pltpu.make_async_remote_copy(
            src_ref=src.at[at], dst_ref=x0.at[at], send_sem=xsend.at[k, child],
            recv_sem=xrecv.at[k], device_id=children[child][1], device_id_type=MESH,
        )

    def each_child(k, what):
        for i, (cond, _) in enumerate(children):
            @pl.when(cond)
            def _(i=i):
                what(xcopy(k, i, x0))

    def xpump(k):
        @pl.when(frame > 0)
        def _():
            xcopy(k, 3, x0).wait_recv()
        each_child(k, lambda d: d.start())

    def kcopy(l, slot, i):
        buf = (kc, vc)[i]
        return pltpu.make_async_remote_copy(
            src_ref=buf.at[l, slot, pl.ds(0, S)], dst_ref=buf.at[l, 1 - slot, pl.ds(2 * S, S)],
            send_sem=ksend.at[l, slot, i], recv_sem=krecv.at[l, 1 - slot, i],
            device_id=ndev, device_id_type=MESH,
        )

    def ksend_slot(l, slot):
        @pl.when(has_next)
        def _():
            kcopy(l, slot, 0).start()
            kcopy(l, slot, 1).start()

        @pl.when(jnp.logical_not(has_prev))
        def _():
            kc[l, slot, 2 * S :, :] = kc[l, slot, :S, :]
            vc[l, slot, 2 * S :, :] = vc[l, slot, :S, :]

    def kwait(l):
        @pl.when(has_prev)
        def _():
            for slot in range(2):
                for i in range(2):
                    kcopy(l, slot, i).wait_recv()

    def project(l, slot, f, only_kv=False):
        w = (qkv_ref, wq)[slot]
        group = mp if slot == 0 else 1 - mp
        a = h[f * S : (f + 1) * S, :]
        lo = R * D if only_kv else 0
        flat = dot(a, w[l, :, lo:])
        if not only_kv:
            for r in range(R):
                t = temp_ref[l, group * R + r] * (1.0 / math.sqrt(D))
                q[f * 6 + slot * R + r] = (head_norm(flat[:, r * D : (r + 1) * D]) * t).astype(BF16)
        kc[l, slot, f * S : (f + 1) * S, :] = head_norm(flat[:, R * D - lo : (R + 1) * D - lo]).astype(BF16)
        vc[l, slot, f * S : (f + 1) * S, :] = flat[:, (R + 1) * D - lo :].astype(BF16)

    col = lax.broadcasted_iota(jnp.int32, (1, 3 * S), 1)
    keep = (col < S) | ((col < 2 * S) & (frame >= 2)) | ((col >= 2 * S) & (frame >= 1))
    bias = jnp.where(keep, 0.0, -1e30).astype(F32)

    def attend(l, f):
        def group(slot, carry):
            for r in range(R):
                qq = q[f * 6 + slot * R + r]
                kk, vv = (kc[l, slot], vc[l, slot]) if f == 0 else (kc[l, slot, S : 2 * S, :], vc[l, slot, S : 2 * S, :])
                s = lax.dot_general(qq, kk, (((1,), (1,)), ((), ())), preferred_element_type=F32)
                if f == 0:
                    s = s + bias
                e = jnp.exp(s - jnp.max(s, axis=-1, keepdims=True))
                total = jnp.sum(e, axis=-1, keepdims=True)
                res = dot(e.astype(BF16), vv) / total
                at = pl.ds(pl.multiple_of((slot * R + r) * D, D), D)
                o[f * S : (f + 1) * S, at] = res.astype(BF16)
            return carry
        lax.fori_loop(0, 2, group, 0)

    half = R * D
    width = up_ref.shape[2]

    def mix(l, f, state):
        rows = slice(f * S, (f + 1) * S)
        upd = dot(o[rows, :half], out_ref[l]) + dot(o[rows, half:], wo[l])
        new = (state.astype(F32) + upd).astype(BF16)
        st[rows, :] = new
        h[rows, :] = norm_rows(new, gf_ref[l : l + 1, :])

    def widen(l, n, slot):
        w = (up_ref, wu)[slot]
        for f in range(n):
            rows = slice(f * S, (f + 1) * S)
            hid = dot(h[rows, :], w[l])
            act[rows, slot * width : (slot + 1) * width] = jax.nn.gelu(hid, approximate=True).astype(BF16)

    def narrow(l, f):
        rows = slice(f * S, (f + 1) * S)
        upd = dot(act[rows, :width], down_ref[l]) + dot(act[rows, width:], wd[l])
        return (st[rows, :].astype(F32) + upd).astype(BF16)

    @pl.when(frame == 0)
    def _():
        x0[...] = x_ref[...]
        for k in range(XCH):
            xpump(k)

    early = jnp.logical_and(chain, frame > 0)
    wcopy(0, 0).start()
    wcopy(1, 0).start()
    h[:S, :] = norm_rows(x_ref[...], ga_ref[0:1, :])
    project(0, 0, 0)
    ksend_slot(0, 0)
    for t in range(3):
        @pl.when(early)
        def _(t=t):
            xpump(t)
        tick(t)

    @pl.when(early)
    def _():
        xpump(3)
    arrived(0)
    project(0, 1, 0)
    ksend_slot(0, 1)
    tick(3)

    @pl.when(jnp.logical_not(chain))
    def _():
        for k in range(XCH):
            xpump(k)
    h[S:, :] = norm_rows(x0[...], ga_ref[0:1, :])
    project(0, 0, 1)
    project(0, 1, 1)
    tick(4)
    attend(0, 1)
    tick(5)
    kwait(0)
    attend(0, 0)
    arrived(1)
    mix(0, 1, x0[...])
    mix(0, 0, x_ref[...])
    tick(6)
    arrived(2)
    widen(0, 2, 0)
    widen(0, 2, 1)
    tick(7)
    arrived(3)
    for f in range(2):
        new = narrow(0, f)
        st[f * S : (f + 1) * S, :] = new
        h[f * S : (f + 1) * S, :] = norm_rows(new, ga_ref[1:2, :])

    arrived(4)
    project(1, 0, 0)
    ksend_slot(1, 0)
    project(1, 1, 0)
    ksend_slot(1, 1)
    tick(8)
    project(1, 0, 1, only_kv=True)
    project(1, 1, 1, only_kv=True)
    tick(9)
    kwait(1)
    attend(1, 0)
    arrived(5)
    mix(1, 0, st[:S, :])
    arrived(6)
    widen(1, 1, 0)
    widen(1, 1, 1)
    arrived(7)
    y_ref[...] = narrow(1, 0)

    for m in range(8):
        for stage in range(4):
            wcopy(m, stage).wait_send()
    for k in range(XCH):
        each_child(k, lambda d: d.wait_send())

    @pl.when(has_next)
    def _():
        for l in range(2):
            for slot in range(2):
                for i in range(2):
                    kcopy(l, slot, i).wait_send()


def solution(mesh):
    T = mesh.shape["tm"]

    def shards(x, ga, qkv, temps, out, gf, up, down):
        width = x.shape[2]
        vmem = pl.BlockSpec(memory_space=pltpu.VMEM)
        smem = pl.BlockSpec(memory_space=pltpu.SMEM)

        def body(*refs):
            kernel(T, *refs)

        y = pl.pallas_call(
            body,
            out_shape=jax.ShapeDtypeStruct((S, width), BF16),
            in_specs=[vmem, vmem, vmem, smem, vmem, vmem, vmem, vmem],
            out_specs=vmem,
            scratch_shapes=[
                pltpu.VMEM(qkv.shape, BF16),
                pltpu.VMEM(out.shape, BF16),
                pltpu.VMEM(up.shape, BF16),
                pltpu.VMEM(down.shape, BF16),
                pltpu.VMEM((S, width), BF16),
                pltpu.VMEM((2 * S, width), BF16),
                pltpu.VMEM((2 * S, width), BF16),
                pltpu.VMEM((12, S, D), BF16),
                pltpu.VMEM((2, 2, 3 * S, D), BF16),
                pltpu.VMEM((2, 2, 3 * S, D), BF16),
                pltpu.VMEM((2 * S, 2 * R * D), BF16),
                pltpu.VMEM((2 * S, 2 * up.shape[2]), BF16),
                pltpu.SemaphoreType.DMA((8, 4)),
                pltpu.SemaphoreType.DMA((8, 4)),
                pltpu.SemaphoreType.DMA((XCH, 4)),
                pltpu.SemaphoreType.DMA((XCH,)),
                pltpu.SemaphoreType.DMA((2, 2, 2)),
                pltpu.SemaphoreType.DMA((2, 2, 2)),
            ],
            compiler_params=pltpu.CompilerParams(
                collective_id=0, has_side_effects=True, vmem_limit_bytes=56 * 1024 * 1024
            ),
        )(x.reshape(S, width), ga, qkv, temps, out, gf, up, down)
        return y.reshape(x.shape)

    in_specs = (
        P(("tm", "mp"), None, None),
        P(),
        P(None, None, "mp"),
        P(),
        P(None, "mp", None),
        P(),
        P(None, None, "mp"),
        P(None, "mp", None),
    )
    return jax.shard_map(
        shards, mesh=mesh, in_specs=in_specs, out_specs=P(("tm", "mp"), None, None), check_vma=False
    )
```

time: 439 us -> 101 us (0.23)
  waiting for transfers between devices: 345 us -> 0 us
  Pallas kernels: 0 us -> 98.6 us
  matrix products: 36.6 us -> 0 us
  other arithmetic: 23.7 us -> 0 us
  between operations: 14.1 us -> 0.01 us
  local copies, waits for them, and re-layouts: 11 us -> 1.92 us
  starting transfers between devices: 5.92 us -> 0 us
    psum x2 -> x0, waiting for transfers between devices: 166 us -> none  [from_root(): return lax.psum(jnp.where(mine, value, jnp.zeros_like(value)), axis)]
    pallas_call x0 -> x1, Pallas kernels: none -> 98.6 us  [shards(): pl.pallas_call(body, out_shape=jax.ShapeDtypeStruct((S, width), BF16), in...]
    reduce_scatter x4 -> x0, waiting for transfers between devices: 90.7 us -> none  [the longest x2 47 us: layer_by_heads(): lax.psum_scatter(jnp.einsum('fsc,cd->fsd', block, out_local, preferred_el...]
    all_gather x4 -> x0, waiting for transfers between devices: 87.1 us -> none  [layer_by_heads(): lax.all_gather(state, 'mp', axis=0, tiled=True)]
    dot_general x18 -> x0, matrix products: 36.6 us -> none  [the longest x2 10.4 us: layer_by_heads(): jnp.einsum('fsc,cd->fsd', block, down_local, preferred_element_type=jnp.f...]
    reduce_sum x10 -> x0, other arithmetic: 10 us -> none  [the longest x4 6.29 us: rms_rows(): jnp.mean(content_vectors * content_vectors, axis=-1, keepdims=True) + 1e-06]
    convert_element_type x8 -> x0, other arithmetic: 9.97 us -> none  [the longest x2 4.03 us: layer_by_heads(): state = (state.astype(jnp.float32) + mixed).astype(jnp.bfloat16)]
    ppermute x4 -> x0, starting transfers between devices: 5.14 us -> none  [passed_along(): return lax.ppermute(value, axis, pairs)]
  transfers between devices with their start and end apart: 14 -> 0, of which waited for: 10 -> 0; matrix products, arithmetic and copies ran while one was open for 5% -> 0% of each run, Pallas kernels for 0% -> 0%
where the time goes in v1:
time: 101 us
  Pallas kernels  98.6 us (98%)
  local copies, waits for them, and re-layouts  1.92 us (2%)
    pallas_call x1, Pallas kernels, shards(): pl.pallas_call(body, out_shape=jax.ShapeDtypeStruct((S, width), BF16), in...  98.6 us

profile of v1, /device:TPU:29, one launch (start us, length us, event | category | flops | bytes accessed | tf_op | source)
XLA Modules:
  0.0 100.5 jit_solution(9953501896935201656)
XLA Ops:
  0.0 98.6 %shard_map.82 = bf16[384,768]{1,0:T(8,128)(2,1)} custom-call(bf16[384,768]{1,0:T(8,128)(2,1)} %bitcast.3, f32[2,768]{1,0:T(2,128)} %refs_1_.1, bf16[2,768,640]{2,1,0:T(8,128)(2,1)} %refs_2_.1, f32[2,6]{1,0:T(2,128)} %refs_3_.1, bf16[2,384,768]{2,1,0:T(8,128)(2,1)} %refs_4_.1, f32[2,768]{1,0:T(2,128)} %refs_5_.1, bf16[2,768,768]{2,1,0:T(8,128)(2,1)} %refs_6_.1, ...), custom_call_target="tpu_custom_call" | custom-call | tf_op jit(solution)/shard_map/pallas_call | solution.py:314
  98.6 1.9 %copy.10 = bf16[1,384,768]{2,1,0:T(8,128)(2,1)} copy(bf16[1,384,768]{2,1,0:T(8,128)(2,1)} %bitcast.2) | data formatting | bytes 1179648

commit v2 on v1

v2 whole, which is shorter than its diff:
```python
import math

import jax
import jax.numpy as jnp
from jax import lax
from jax.experimental import pallas as pl
from jax.experimental.pallas import tpu as pltpu
from jax.sharding import PartitionSpec as P

D = 128
R = 3
S = 384
XCH = 4
MESH = pl.DeviceIdType.MESH
F32, BF16 = jnp.float32, jnp.bfloat16


def norm_rows(x, gain):
    x = x.astype(F32)
    scale = lax.rsqrt(jnp.mean(x * x, axis=-1, keepdims=True) + 1e-06)
    return (x * scale * gain).astype(BF16)


def head_norm(t):
    return t * lax.rsqrt(jnp.mean(t * t, axis=-1, keepdims=True) + 1e-06)


def dot(a, b):
    return jnp.dot(a, b, preferred_element_type=F32)


def kernel(
    T,
    x_ref, ga_ref, qkv_hbm, temp_ref, out_hbm, gf_ref, up_hbm, down_hbm,
    y_ref,
    qkv_ref, out_ref, up_ref, down_ref, wq, wo, wu, wd,
    x0, st, h, q, kc, vc, o, act, top, total, acc,
    loaded, ws, wr, xsend, xrecv, ksend, krecv, asend, arecv,
):
    tm, mp = lax.axis_index("tm"), lax.axis_index("mp")
    c, yb, zb = lax.rem(tm, 2), lax.rem(tm // 2, 2), lax.rem(tm // 4, 2)
    frame = tm * 2 + mp
    xdev = (tm, 1 - mp)
    cdev = (tm + 1 - 2 * c, mp)
    ydev = (tm + 2 - 4 * yb, mp)
    zdev = (tm + 4 - 8 * zb, mp)
    has_next = frame < 2 * T - 1
    has_prev = frame > 0
    ndev = (jnp.minimum(tm + mp, T - 1), 1 - mp)
    chain = jnp.logical_and(lax.rem(tm, 4) == 0, mp == 0)
    chain_next = jnp.logical_and(chain, tm + 4 < T)
    znext = jnp.minimum(tm + 4, T - 4)

    for m in range(8):
        src, dst, l = ((qkv_hbm, qkv_ref), (out_hbm, out_ref), (up_hbm, up_ref), (down_hbm, down_ref))[m % 4] + (m // 4,)
        pltpu.make_async_copy(src.at[l], dst.at[l], loaded.at[m]).start()

    barrier = pltpu.get_barrier_semaphore()
    for dev in (xdev, cdev, ydev, zdev):
        pl.semaphore_signal(barrier, inc=1, device_id=dev, device_id_type=MESH)
    diag_up = jnp.logical_and(mp == 1, tm < T - 1)
    diag_down = jnp.logical_and(mp == 0, tm > 0)
    z_up = jnp.logical_and(jnp.logical_and(chain, zb == 1), tm + 4 < T)
    z_down = jnp.logical_and(jnp.logical_and(chain, zb == 0), tm > 0)

    def greet(cond, dev):
        @pl.when(cond)
        def _():
            pl.semaphore_signal(barrier, inc=1, device_id=dev, device_id_type=MESH)

    greet(diag_up, (jnp.minimum(tm + 1, T - 1), 0))
    greet(diag_down, (jnp.maximum(tm - 1, 0), 1))
    greet(z_up, (znext, 0))
    greet(z_down, (jnp.maximum(tm - 4, 0), 0))
    peers = jnp.int32(4)
    for cond in (diag_up, diag_down, z_up, z_down):
        peers = peers + jnp.where(cond, 1, 0)
    pl.semaphore_wait(barrier, peers)

    mats = []
    for l in range(2):
        mats += [(qkv_hbm, wq, l), (out_hbm, wo, l), (up_hbm, wu, l), (down_hbm, wd, l)]
    held = (qkv_ref, out_ref, up_ref, down_ref)

    def load(m):
        src, _, l = mats[m]
        return pltpu.make_async_copy(src.at[l], held[m % 4].at[l], loaded.at[m])

    def wcopy(m, stage):
        src, dst, l = mats[m]
        rows = dst.shape[1] // 8
        y_first = m % 2 == 0
        e = c * 4 + (zb * 2 + yb if y_first else yb * 2 + zb)
        if stage == 0:
            at = pl.ds(pl.multiple_of(e * rows, rows), rows)
            sref, dev = src.at[l, at], xdev
        else:
            n = (0, 1, 2, 4)[stage]
            lead = (e, e, c * 4 + (zb if y_first else yb) * 2, c * 4)[stage]
            at = pl.ds(pl.multiple_of(lead * rows, rows), n * rows)
            sref = dst.at[l, at]
            dev = (None, ydev if y_first else zdev, zdev if y_first else ydev, cdev)[stage]
        return pltpu.make_async_remote_copy(
            src_ref=sref, dst_ref=dst.at[l, at], send_sem=ws.at[m, stage],
            recv_sem=wr.at[m, stage], device_id=dev, device_id_type=MESH,
        )

    def tick(t):
        if t + 2 < 8:
            wcopy(t + 2, 0).start()
        for stage in (1, 2, 3):
            m = t + 1 - stage
            if 0 <= m < 8:
                wcopy(m, stage - 1).wait_recv()
                wcopy(m, stage).start()

    def arrived(m):
        wcopy(m, 3).wait_recv()

    step = S // XCH
    children = (
        (chain_next, (znext, 0)),
        (chain, (tm + 2 - 4 * yb, 0)),
        (jnp.logical_and(c == 0, mp == 0), (tm, 1)),
        (c == 0, cdev),
    )

    def xcopy(k, child, src):
        at = pl.ds(k * step, step)
        return pltpu.make_async_remote_copy(
            src_ref=src.at[at], dst_ref=x0.at[at], send_sem=xsend.at[k, child],
            recv_sem=xrecv.at[k], device_id=children[child][1], device_id_type=MESH,
        )

    def each_child(make, what):
        for i, (cond, _) in enumerate(children):
            @pl.when(cond)
            def _(i=i):
                what(make(i))

    def xpump(k):
        @pl.when(frame > 0)
        def _():
            xcopy(k, 3, x0).wait_recv()
        each_child(lambda i: xcopy(k, i, x0), lambda d: d.start())

    def acopy(piece, child):
        g, buf = piece // 2, (kc, vc)[piece % 2]
        here = g + mp - 2 * g * mp
        there = 1 - here if child == 2 else here
        at = pl.ds(S, S)
        return pltpu.make_async_remote_copy(
            src_ref=buf.at[1, here, at], dst_ref=buf.at[1, there, at], send_sem=asend.at[piece, child],
            recv_sem=arecv.at[piece], device_id=children[child][1], device_id_type=MESH,
        )

    def apump(piece):
        @pl.when(frame > 0)
        def _():
            acopy(piece, 3).wait_recv()
        each_child(lambda i: acopy(piece, i), lambda d: d.start())

    def kcopy(l, slot, i):
        buf = (kc, vc)[i]
        return pltpu.make_async_remote_copy(
            src_ref=buf.at[l, slot, pl.ds(0, S)], dst_ref=buf.at[l, 1 - slot, pl.ds(2 * S, S)],
            send_sem=ksend.at[l, slot, i], recv_sem=krecv.at[l, 1 - slot, i],
            device_id=ndev, device_id_type=MESH,
        )

    def ksend_slot(l, slot):
        @pl.when(has_next)
        def _():
            kcopy(l, slot, 0).start()
            kcopy(l, slot, 1).start()

    def kwait(l, slot):
        @pl.when(has_prev)
        def _():
            for i in range(2):
                kcopy(l, 1 - slot, i).wait_recv()

    def project(l, slot, f, only_kv=False, h0=None):
        w = (qkv_ref, wq)[slot]
        group = mp if slot == 0 else 1 - mp
        a = h[...] if f == 0 else h0
        lo = R * D if only_kv else 0
        flat = dot(a, w[l, :, lo:])
        if not only_kv:
            for r in range(R):
                t = temp_ref[l, group * R + r] * (1.0 / math.sqrt(D))
                q[slot * R + r] = (head_norm(flat[:, r * D : (r + 1) * D]) * t).astype(BF16)
        kc[l, slot, f * S : (f + 1) * S, :] = head_norm(flat[:, R * D - lo : (R + 1) * D - lo]).astype(BF16)
        vc[l, slot, f * S : (f + 1) * S, :] = flat[:, (R + 1) * D - lo :].astype(BF16)

    col = lax.broadcasted_iota(jnp.int32, (1, 2 * S), 1)
    bias = jnp.where((col >= S) | (frame >= 2), 0.0, -1e30).astype(F32)

    def scores(qq, kk):
        return lax.dot_general(qq, kk, (((1,), (1,)), ((), ())), preferred_element_type=F32)

    def own_part(l, slot):
        kk, vv = kc[l, slot, :S, :], vc[l, slot, :S, :]
        for r in range(R):
            i = slot * R + r
            s = scores(q[i], kk)
            m = jnp.max(s, axis=-1, keepdims=True)
            e = jnp.exp(s - m)
            top[i] = m
            total[i] = jnp.sum(e, axis=-1, keepdims=True)
            acc[i] = dot(e.astype(BF16), vv)

    def other_part(l, slot):
        @pl.when(has_prev)
        def _():
            kk, vv = kc[l, slot, S:, :], vc[l, slot, S:, :]
            for r in range(R):
                i = slot * R + r
                s = scores(q[i], kk) + bias
                m = jnp.maximum(top[i], jnp.max(s, axis=-1, keepdims=True))
                e = jnp.exp(s - m)
                keep = jnp.exp(top[i] - m)
                sums = total[i] * keep + jnp.sum(e, axis=-1, keepdims=True)
                res = (acc[i] * keep + dot(e.astype(BF16), vv)) / sums
                o[:, i * D : (i + 1) * D] = res.astype(BF16)

        @pl.when(jnp.logical_not(has_prev))
        def _():
            for r in range(R):
                i = slot * R + r
                o[:, i * D : (i + 1) * D] = (acc[i] / total[i]).astype(BF16)

    half = R * D
    width = up_ref.shape[2]

    def mix(l, state):
        upd = dot(o[:, :half], out_ref[l]) + dot(o[:, half:], wo[l])
        new = (state.astype(F32) + upd).astype(BF16)
        st[...] = new
        h[...] = norm_rows(new, gf_ref[l : l + 1, :])

    def widen(l, slot):
        w = (up_ref, wu)[slot]
        hid = dot(h[...], w[l])
        act[:, slot * width : (slot + 1) * width] = jax.nn.gelu(hid, approximate=True).astype(BF16)

    def narrow(l):
        upd = dot(act[:, :width], down_ref[l]) + dot(act[:, width:], wd[l])
        return (st[...].astype(F32) + upd).astype(BF16)

    @pl.when(frame == 0)
    def _():
        x0[...] = x_ref[...]
        for k in range(XCH):
            xpump(k)

    early = jnp.logical_and(chain, frame > 0)
    late = jnp.logical_not(chain)
    wcopy(0, 0).start()
    wcopy(1, 0).start()
    h[...] = norm_rows(x_ref[...], ga_ref[0:1, :])
    load(0).wait()
    project(0, 0, 0)
    ksend_slot(0, 0)
    for t in range(3):
        @pl.when(early)
        def _(t=t):
            xpump(t)
        tick(t)
        if t == 0:
            own_part(0, 0)

    @pl.when(early)
    def _():
        xpump(3)
    arrived(0)
    project(0, 1, 0)
    ksend_slot(0, 1)
    tick(3)

    @pl.when(late)
    def _():
        xpump(0)
        xpump(1)
    own_part(0, 1)

    @pl.when(late)
    def _():
        xpump(2)
        xpump(3)
    tick(4)

    @pl.when(has_prev)
    def _():
        h0 = norm_rows(x0[...], ga_ref[0:1, :])
        project(0, 0, 1, only_kv=True, h0=h0)
        project(0, 1, 1, only_kv=True, h0=h0)
    kwait(0, 0)
    kwait(0, 1)
    tick(5)
    other_part(0, 0)
    tick(6)
    other_part(0, 1)
    load(1).wait()
    arrived(1)
    mix(0, x_ref[...])
    load(2).wait()
    widen(0, 0)
    tick(7)
    arrived(2)
    widen(0, 1)
    load(3).wait()
    arrived(3)
    new = narrow(0)
    st[...] = new
    h[...] = norm_rows(new, ga_ref[1:2, :])

    load(4).wait()
    project(1, 0, 0)
    ksend_slot(1, 0)

    @pl.when(frame == 0)
    def _():
        kc[1, 0, S : 2 * S, :] = kc[1, 0, :S, :]
        vc[1, 0, S : 2 * S, :] = vc[1, 0, :S, :]
        apump(0)
        apump(1)
    arrived(4)
    project(1, 1, 0)
    ksend_slot(1, 1)

    @pl.when(frame == 0)
    def _():
        kc[1, 1, S : 2 * S, :] = kc[1, 1, :S, :]
        vc[1, 1, S : 2 * S, :] = vc[1, 1, :S, :]
        apump(2)
        apump(3)
    tick(8)

    @pl.when(early)
    def _():
        apump(0)
        apump(1)
    own_part(1, 0)

    @pl.when(early)
    def _():
        apump(2)
        apump(3)

    @pl.when(late)
    def _():
        apump(0)
        apump(1)
    tick(9)
    own_part(1, 1)

    @pl.when(late)
    def _():
        apump(2)
        apump(3)
    kwait(1, 0)
    other_part(1, 0)
    kwait(1, 1)
    other_part(1, 1)
    load(5).wait()
    arrived(5)
    mix(1, st[...])
    load(6).wait()
    widen(1, 0)
    arrived(6)
    widen(1, 1)
    load(7).wait()
    arrived(7)
    y_ref[...] = narrow(1)

    for m in range(8):
        for stage in range(4):
            wcopy(m, stage).wait_send()
    for k in range(XCH):
        each_child(lambda i, k=k: xcopy(k, i, x0), lambda d: d.wait_send())
    for piece in range(4):
        each_child(lambda i, piece=piece: acopy(piece, i), lambda d: d.wait_send())

    @pl.when(has_next)
    def _():
        for l in range(2):
            for slot in range(2):
                for i in range(2):
                    kcopy(l, slot, i).wait_send()


def solution(mesh):
    T = mesh.shape["tm"]

    def shards(x, ga, qkv, temps, out, gf, up, down):
        width = x.shape[2]
        vmem = pl.BlockSpec(memory_space=pltpu.VMEM)
        hbm = pl.BlockSpec(memory_space=pl.ANY)
        smem = pl.BlockSpec(memory_space=pltpu.SMEM)

        def body(*refs):
            kernel(T, *refs)

        y = pl.pallas_call(
            body,
            out_shape=jax.ShapeDtypeStruct((S, width), BF16),
            in_specs=[vmem, vmem, hbm, smem, hbm, vmem, hbm, hbm],
            out_specs=vmem,
            scratch_shapes=[
                *[pltpu.VMEM(w.shape, BF16) for w in (qkv, out, up, down)] * 2,
                pltpu.VMEM((S, width), BF16),
                pltpu.VMEM((S, width), BF16),
                pltpu.VMEM((S, width), BF16),
                pltpu.VMEM((2 * R, S, D), BF16),
                pltpu.VMEM((2, 2, 3 * S, D), BF16),
                pltpu.VMEM((2, 2, 3 * S, D), BF16),
                pltpu.VMEM((S, 2 * R * D), BF16),
                pltpu.VMEM((S, 2 * up.shape[2]), BF16),
                pltpu.VMEM((2 * R, S, 1), F32),
                pltpu.VMEM((2 * R, S, 1), F32),
                pltpu.VMEM((2 * R, S, D), F32),
                pltpu.SemaphoreType.DMA((8,)),
                pltpu.SemaphoreType.DMA((8, 4)),
                pltpu.SemaphoreType.DMA((8, 4)),
                pltpu.SemaphoreType.DMA((XCH, 4)),
                pltpu.SemaphoreType.DMA((XCH,)),
                pltpu.SemaphoreType.DMA((2, 2, 2)),
                pltpu.SemaphoreType.DMA((2, 2, 2)),
                pltpu.SemaphoreType.DMA((4, 4)),
                pltpu.SemaphoreType.DMA((4,)),
            ],
            compiler_params=pltpu.CompilerParams(
                collective_id=0, has_side_effects=True, vmem_limit_bytes=56 * 1024 * 1024
            ),
        )(x.reshape(S, width), ga, qkv, temps, out, gf, up, down)
        return y.reshape(x.shape)

    in_specs = (
        P(("tm", "mp"), None, None),
        P(),
        P(None, None, "mp"),
        P(),
        P(None, "mp", None),
        P(),
        P(None, None, "mp"),
        P(None, "mp", None),
    )
    return jax.shard_map(
        shards, mesh=mesh, in_specs=in_specs, out_specs=P(("tm", "mp"), None, None), check_vma=False
    )
```

time: 101 us -> 99 us (0.980)
  the two profiles are of different devices: /device:TPU:29 before, /device:TPU:31 now
where the time goes in v2:
time: 99 us; the launch traced here: 98.9 us
  Pallas kernels  96.9 us (98%)
  local copies, waits for them, and re-layouts  1.92 us (2%)
    pallas_call x1, Pallas kernels, shards(): pl.pallas_call(body, out_shape=jax.ShapeDtypeStruct((S, width), BF16), in...  96.9 us

profile of v2, /device:TPU:31, one launch (start us, length us, event | category | flops | bytes accessed | tf_op | source)
XLA Modules:
  0.0 98.9 jit_solution(16735826137752824239)
XLA Ops:
  0.0 96.9 %shard_map.82 = bf16[384,768]{1,0:T(8,128)(2,1)} custom-call(bf16[384,768]{1,0:T(8,128)(2,1)} %bitcast.3, f32[2,768]{1,0:T(2,128)} %refs_1_.1, bf16[2,768,640]{2,1,0:T(8,128)(2,1)} %refs_2_.1, f32[2,6]{1,0:T(2,128)} %refs_3_.1, bf16[2,384,768]{2,1,0:T(8,128)(2,1)} %refs_4_.1, f32[2,768]{1,0:T(2,128)} %refs_5_.1, bf16[2,768,768]{2,1,0:T(8,128)(2,1)} %refs_6_.1, ...), custom_call_target="tpu_custom_call" | custom-call | tf_op jit(solution)/shard_map/pallas_call | solution.py:405
  96.9 1.9 %copy.10 = bf16[1,384,768]{2,1,0:T(8,128)(2,1)} copy(bf16[1,384,768]{2,1,0:T(8,128)(2,1)} %bitcast.2) | data formatting | bytes 1179648
